TPU v7x, 256 devices: a whole 4x4x8 slice. The times are simulated.
256 devices in a mesh: seq: 16 (over z_hi, x), tp: 16 (over z_lo, y, core).
Axes of the slice: x: 4, y: 4, z: 8 (z_hi: 4, z_lo: 2; z = z_hi * 2 + z_lo), core: 2. Of those that a mesh axis runs over, the one named last changes fastest.
Arguments:
- teacher_attn: bfloat16 [2048, 16384], P('seq', 'tp'), may hold values from -6 to 6
- teacher_out_w: bfloat16 [16384, 16384], P('tp', 'seq'), may hold values from -0.046875 to 0.046875
- teacher_resid: bfloat16 [2048, 16384], P(None, 'seq')
- teacher_gain: float32 [16384], P('seq'), may hold values from 0.1 to 1.9
- projector: bfloat16 [16384, 8192], P('seq', 'tp'), may hold values from -0.046875 to 0.046875
- student_attn: bfloat16 [2048, 8192], P('tp', 'seq'), may hold values from -6 to 6
- student_out_w: bfloat16 [8192, 8192], P('seq', 'tp'), may hold values from -0.0625 to 0.0625
- student_resid: bfloat16 [2048, 8192], P('seq', 'tp')
Outputs:
- mse: float32 [], replicated
- grad_student_w: float32 [8192, 8192], P('seq', 'tp')
- grad_projector: float32 [16384, 8192], P('seq', 'tp')
All inputs are finite; a program needn't handle non-finite values.
Results may differ from a plain program's by a relative error of at most 0.025.
Values may be sent and summed in bfloat16 or wider, within the bound.
A program may use at most 64 MiB of HBM per device.

v0:
```python
import functools

import jax
import jax.numpy as jnp
from jax import lax
from jax.experimental import pallas as pl
from jax.experimental.pallas import tpu as pltpu
from jax.sharding import PartitionSpec as P

MESH = pl.DeviceIdType.MESH
BF = jnp.bfloat16
F32 = jnp.float32

DT = 16384
DS = 8192
EPSILON = 1e-05
LOSS_SCALE = 32.0

SIZES = (16, 16, 16, 16, 16, 16, 16, 16)
NC = len(SIZES)
STARTS = tuple(sum(SIZES[:c]) for c in range(NC))
ROWS = 128
TOKENS = 2048
KT = 1024
KS = 512
TILE = 256
GAP_STAGE = 14

PER_CHUNK = {
    "az": 3, "ao": 2, "ag": 2, "ax": 2, "af": 2,
    "tc": 1, "ty": 3, "tz": 1,
    "pz": 3, "px": 3, "iy": 3, "ic": 1,
    "ny": 3, "nc": 1,
    "gx": 3, "gz": 3,
    "ez": 3, "ex": 3,
}
ONCE = {"sz": 1, "sy": 3, "sf": 3, "sc": 1, "mz": 3, "mx": 3, "my": 3, "ml": 1, "mc": 1}
BASE = {}
TOTAL = 0
for _name, _count in PER_CHUNK.items():
    BASE[_name] = TOTAL
    TOTAL += _count * NC
for _name, _count in ONCE.items():
    BASE[_name] = TOTAL
    TOTAL += _count
LOADS = 9

ORDER = (
    0, 1, 1, 0, 0, 2, 0, 1, 3, 2, 0, 2, 4, 0, 1, 3, 3, 5, 2, 4, 1, 0, 4, 6, 1, 3, 5, 5, 7, 2, 0, 2,
    6, 4, 1, 3, 6, 3, 5, 7, 7, 1, 4, 0, 2, 6, 4, 5, 1, 3, 5, 7, 2, 0, 0, 3, 1, 1, 6, 2, 4, 7, 3, 5,
    6, 2, 7, 4, 0, 2, 3, 5, 0, 1, 3, 4, 1, 2, 5, 6, 7, 0, 2, 6, 1, 3, 4, 4, 5, 7, 3, 0, 1, 2, 4, 5,
    5, 6, 7, 4, 5, 1, 3, 6, 0, 2, 6, 7, 7, 4, 6, 6, 2, 3, 7, 5, 4, 7, 1, 3, 5, 6, 0, 2, 7, 5, 6, 4,
    3, 7, 6, 5, 7, 4, 6, 7,
)
GATHER_AT = (0, 2, 5, 11)


def kernel(
    ta, w1_hbm, tr, gain_hbm, pj_hbm, sa_hbm, sw_hbm, sr_hbm,
    mse_ref, gs, gp,
    w1, pj, sw, gain, res, sr,
    a_all, cs, cr, own1, qs, yr, zs, zr, psz, psx, inv_all,
    h_all, n_all, s_all, g_part, xr, e_wide, es, er, e_all,
    ms, mz, mx, my, ml, mc,
    send, recv, load,
):
    s = lax.axis_index("seq")
    t = lax.axis_index("tp")
    zh, x = s // 4, s % 4
    zl, y, co = t // 8, (t // 2) % 4, t % 2
    zlp, cop = 1 - zl, 1 - co

    def at(zh_, x_, zl_, y_, co_):
        return (zh_ * 4 + x_, zl_ * 8 + y_ * 2 + co_)

    def zh_dev(d):
        return at((zh + d) % 4, x, zl, y, co)

    def x_dev(d):
        return at(zh, (x + d) % 4, zl, y, co)

    def y_dev(d):
        return at(zh, x, zl, (y + d) % 4, co)

    zl_dev = at(zh, x, zlp, y, co)
    co_dev = at(zh, x, zl, y, cop)

    started = []

    def index_of(name, c, i):
        return BASE[name] + (c * PER_CHUNK[name] if name in PER_CHUNK else 0) + i

    def push(name, c, i, src, dst, dev):
        k = index_of(name, c, i)
        copy = pltpu.make_async_remote_copy(
            src_ref=src, dst_ref=dst, send_sem=send.at[k], recv_sem=recv.at[k],
            device_id=dev, device_id_type=MESH,
        )
        copy.start()
        started.append(copy)

    def landed(name, c, i, where):
        k = index_of(name, c, i)
        pltpu.make_async_remote_copy(
            src_ref=where, dst_ref=where, send_sem=send.at[k], recv_sem=recv.at[k],
            device_id=co_dev, device_id_type=MESH,
        ).wait_recv()

    loads = []
    waited = set()

    def ready(*copies):
        for copy in copies:
            if id(copy) not in waited:
                waited.add(id(copy))
                copy.wait()

    def fetch(src, dst):
        copy = pltpu.make_async_copy(src, dst, load.at[len(loads)])
        copy.start()
        loads.append(copy)
        return copy

    def rows(c):
        return pl.ds(STARTS[c], SIZES[c])

    def a_at(c, d, x_, cols=slice(None)):
        return a_all.at[d, x_ // 2, x_ % 2, rows(c), cols]

    own_a = fetch(ta, a_all.at[0, x // 2, x % 2])
    own_s = fetch(sa_hbm, s_all.at[zl, y, co])
    get_w1 = fetch(w1_hbm, w1)
    get_res = fetch(tr.at[:, y * 2 + co], res)
    get_gain = fetch(gain_hbm, gain)
    get_sw = fetch(sw_hbm, sw)
    get_pj = fetch(pj_hbm, pj)
    get_sr = fetch(sr_hbm, sr)

    barrier = pltpu.get_barrier_semaphore()
    peers = [zh_dev(d) for d in (1, 2, 3)] + [x_dev(d) for d in (1, 2, 3)]
    peers += [y_dev(d) for d in (1, 2, 3)] + [zl_dev, co_dev]
    for dev in peers:
        pl.semaphore_signal(barrier, inc=1, device_id=dev, device_id_type=MESH)
    pl.semaphore_wait(barrier, len(peers))

    tile_row = lax.broadcasted_iota(jnp.int32, (8, 128), 0)

    def diagonal(c):
        shape = (SIZES[c], 128)
        return lax.broadcasted_iota(jnp.int32, shape, 0) == lax.broadcasted_iota(jnp.int32, shape, 1)


    xp, xm, xo = (x + 1) % 4, (x + 3) % 4, (x + 2) % 4

    def student_gather():
        for d in (1, 2, 3):
            push("sy", 0, d - 1, sa_hbm, s_all.at[zl, y, co], y_dev(d))
        push("sz", 0, 0, sa_hbm, s_all.at[zl, y, co], zl_dev)
        yield
        landed("sz", 0, 0, s_all.at[zlp, y, co])
        for d in (1, 2, 3):
            push("sf", 0, d - 1, s_all.at[zlp, y, co], s_all.at[zlp, y, co], y_dev(d))
        yield
        ready(own_s)
        for d in (1, 2, 3):
            y_ = (y + 4 - d) % 4
            landed("sy", 0, d - 1, s_all.at[zl, y_, co])
            landed("sf", 0, d - 1, s_all.at[zlp, y_, co])
        push("sc", 0, 0, s_all.at[:, :, co], s_all.at[:, :, co], co_dev)
        yield
        landed("sc", 0, 0, s_all.at[:, :, cop])
        yield

    def chunk(c):
        size = SIZES[c]
        at_c = rows(c)
        left_cols, right_cols = pl.ds(0, KT // 2), pl.ds(KT // 2, KT // 2)
        rest = pl.ds(1, 3)
        source = ta.at[at_c]
        for d in (1, 3, 2):
            push("az", c, d - 1, source, a_at(c, d, x), zh_dev(d))
        push("ao", c, 0, source, a_at(c, 0, x), x_dev(1))
        push("ao", c, 1, source, a_at(c, 0, x), x_dev(3))
        yield
        landed("ao", c, 0, a_at(c, 0, xm))
        far = a_at(c, 0, xm, left_cols)
        push("ag", c, 0, far, far, x_dev(1))
        landed("ao", c, 1, a_at(c, 0, xp))
        far = a_at(c, 0, xp, right_cols)
        push("ag", c, 1, far, far, x_dev(3))
        yield
        for d in (1, 3, 2):
            landed("az", c, d - 1, a_at(c, d, x))
        push("ax", c, 0, a_at(c, rest, x), a_at(c, rest, x), x_dev(1))
        push("ax", c, 1, a_at(c, rest, x), a_at(c, rest, x), x_dev(3))
        yield
        landed("ax", c, 0, a_at(c, rest, xm))
        far = a_at(c, rest, xm, left_cols)
        push("af", c, 0, far, far, x_dev(1))
        landed("ax", c, 1, a_at(c, rest, xp))
        far = a_at(c, rest, xp, right_cols)
        push("af", c, 1, far, far, x_dev(3))
        yield
        landed("ag", c, 0, a_at(c, 0, xo, left_cols))
        landed("ag", c, 1, a_at(c, 0, xo, right_cols))
        landed("af", c, 0, a_at(c, rest, xo, left_cols))
        landed("af", c, 1, a_at(c, rest, xo, right_cols))
        ready(own_a, get_w1)

        def z_places(d):
            return pl.ds((zh + 4 - d) % 4 * 2, 2)

        other = a_all[:, :, cop, at_c, :].reshape(8 * size, KT)
        for n in range(KT // TILE):
            cols = pl.ds(n * TILE, TILE)
            part = jnp.dot(other, w1[:, cols], preferred_element_type=F32)
            part = part.astype(BF).reshape(4, 2, size, TILE)
            for d in range(4):
                cs[z_places(d), at_c, cols] = part[d]
        push("tc", c, 0, cs.at[:, at_c], cr.at[:, at_c], co_dev)
        own = a_all[:, :, co, at_c, :].reshape(8 * size, KT)
        for n in range(KT // TILE):
            cols = pl.ds(n * TILE, TILE)
            part = jnp.dot(own, w1[:, cols], preferred_element_type=F32)
            part = part.reshape(4, 2, size, TILE)
            for d in range(4):
                own1[z_places(d), at_c, cols] = part[d]
        yield
        landed("tc", c, 0, cr.at[:, at_c])
        for k in range(8):
            both = own1[k, at_c] + cr[k, at_c].astype(F32)
            own1[k, at_c] = both
            qs[k // 4, k % 4, at_c] = both.astype(BF)
        for d in (1, 3, 2):
            push("ty", c, d - 1, qs.at[:, (y + d) % 4, at_c], yr.at[d - 1, :, at_c], y_dev(d))
        yield
        for d in (1, 3, 2):
            landed("ty", c, d - 1, yr.at[d - 1, :, at_c])
        for k in range(2):
            both = own1[k * 4 + y, at_c]
            for d in range(3):
                both = both + yr[d, k, at_c].astype(F32)
            zs[k, at_c] = both.astype(BF)
        push("tz", c, 0, zs.at[:, at_c], zr.at[:, at_c], zl_dev)
        yield
        landed("tz", c, 0, zr.at[:, at_c])
        ready(get_res)
        lines = []
        for k in range(2):
            total = zs[k, at_c].astype(F32) + zr[k, at_c].astype(F32)
            hidden = (res[k, at_c].astype(F32) + total).astype(BF)
            h_all[k, y, co, at_c] = hidden
            wide = hidden.astype(F32)
            squares = jnp.sum(wide * wide, axis=1, keepdims=True)
            lines.append(jnp.sum(jnp.where(diagonal(c), squares, 0.0), axis=0, keepdims=True))
        psz[c, zh] = jnp.where(tile_row == 0, lines[0], jnp.where(tile_row == 1, lines[1], 0.0))
        for d in (1, 3, 2):
            push("pz", c, d - 1, psz.at[c, zh], psz.at[c, zh], zh_dev(d))
        block = h_all.at[:, y, co, at_c]
        for d in (1, 3, 2):
            push("ny", c, d - 1, block, block, y_dev(d))
        yield
        for d in (1, 3, 2):
            landed("pz", c, d - 1, psz.at[c, (zh + 4 - d) % 4])
        psx[c, x] = psz[c, 0] + psz[c, 1] + psz[c, 2] + psz[c, 3]
        for d in (1, 3, 2):
            push("px", c, d - 1, psx.at[c, x], psx.at[c, x], x_dev(d))
        yield
        for d in (1, 3, 2):
            landed("px", c, d - 1, psx.at[c, (x + 4 - d) % 4])
        line = psx[c, 0] + psx[c, 1] + psx[c, 2] + psx[c, 3]
        inv_all[c, y, co] = lax.rsqrt(line / DT + EPSILON)
        block = inv_all.at[c, y, co]
        for d in (1, 3, 2):
            push("iy", c, d - 1, block, block, y_dev(d))
        yield
        for d in (1, 3, 2):
            landed("ny", c, d - 1, h_all.at[:, (y + 4 - d) % 4, co, at_c])
        block = h_all.at[:, :, co, at_c]
        push("nc", c, 0, block, block, co_dev)
        yield
        for d in (1, 3, 2):
            landed("iy", c, d - 1, inv_all.at[c, (y + 4 - d) % 4, co])
        block = inv_all.at[c, :, co]
        push("ic", c, 0, block, block, co_dev)
        yield
        landed("nc", c, 0, h_all.at[:, :, cop, at_c])
        landed("ic", c, 0, inv_all.at[c, :, cop])
        ready(get_gain, get_pj, get_sw)
        for _ in gather:
            pass

        def norm(k, carry):
            for core in range(2):
                inv = inv_all[c, k, core]
                for z_ in range(2):
                    line = jnp.broadcast_to(inv[z_ : z_ + 1, :], (size, 128))
                    column = jnp.sum(jnp.where(diagonal(c), line, 0.0), axis=1, keepdims=True)
                    wide = h_all[z_, k, core, at_c].astype(F32)
                    n_all[z_, k, core, at_c] = (wide * column * gain[...]).astype(BF)
            return carry

        lax.fori_loop(0, 4, norm, 0)
        for m in range(2):
            half = n_all[m, :, :, at_c, :].reshape(8 * size, KT)
            s_half = s_all[m, :, :, at_c, :].reshape(8 * size, KS)
            for n in range(KS // TILE):
                cols = pl.ds(n * TILE, TILE)
                part = jnp.dot(s_half, sw[:, cols], preferred_element_type=F32)
                part = part - jnp.dot(half, pj[:, cols], preferred_element_type=F32)
                g_part[pl.ds(m * 2, 2), :, at_c, cols] = part.astype(BF).reshape(2, 4, size, TILE)
        for d in (1, 3, 2):
            push("gx", c, d - 1, g_part.at[:, (x + d) % 4, at_c], xr.at[d - 1, :, at_c], x_dev(d))
        yield
        for d in (1, 3, 2):
            landed("gx", c, d - 1, xr.at[d - 1, :, at_c])
        for k in range(4):
            both = g_part[k, x, at_c].astype(F32)
            for d in range(3):
                both = both + xr[d, k, at_c].astype(F32)
            e_wide[k, at_c] = both
            es[k, at_c] = both.astype(BF)
        for d in (1, 3, 2):
            push("gz", c, d - 1, es.at[(zh + d) % 4, at_c], er.at[d - 1, at_c], zh_dev(d))
        yield
        for d in (1, 3, 2):
            landed("gz", c, d - 1, er.at[d - 1, at_c])
        ready(get_sr)
        gap = e_wide[zh, at_c]
        for d in range(3):
            gap = gap + er[d, at_c].astype(F32)
        gap = gap + sr[at_c].astype(F32)
        squared = jnp.sum((gap * gap).reshape(size // 8, 8, KS), axis=0)
        ms[c] = sum(squared[:, 128 * k : 128 * (k + 1)] for k in range(KS // 128))
        if c == final:
            next(mse_steps)
        e_all[zh, x, at_c] = (LOSS_SCALE / TOKENS * gap).astype(BF)
        block = e_all.at[zh, x, at_c]
        for d in (1, 3, 2):
            push("ez", c, d - 1, block, block, zh_dev(d))
        yield
        if c == final:
            next(mse_steps)
            next(mse_steps)
        for d in (1, 3, 2):
            landed("ez", c, d - 1, e_all.at[(zh + 4 - d) % 4, x, at_c])
        block = e_all.at[:, x, at_c]
        for d in (1, 3, 2):
            push("ex", c, d - 1, block, block, x_dev(d))
        if c == final:
            next(mse_steps)
        yield
        for d in (1, 3, 2):
            landed("ex", c, d - 1, e_all.at[:, (x + 4 - d) % 4, at_c])
        if c == final:
            next(mse_steps)
        error = e_all[:, :, at_c, :].reshape(16 * size, KS)
        over_rows = (((0,), (0,)), ((), ()))
        for m in range(KS // TILE):
            cols = pl.ds(m * TILE, TILE)
            left = s_all[:, :, :, at_c, cols].reshape(16 * size, TILE)
            part = lax.dot_general(left, error, over_rows, preferred_element_type=F32)
            gs[cols, :] = part if first_grad[0] else gs[cols, :] + part
        for m in range(KT // TILE):
            cols = pl.ds(m * TILE, TILE)
            left = n_all[:, :, :, at_c, cols].reshape(16 * size, TILE)
            part = lax.dot_general(left, error, over_rows, preferred_element_type=F32)
            gp[cols, :] = -part if first_grad[0] else gp[cols, :] - part
        first_grad[0] = False
        yield

    def squared_total():
        my[y] = sum(ms[c] for c in range(NC))
        for d in (1, 2, 3):
            push("my", 0, d - 1, my.at[y], my.at[y], y_dev(d))
        yield
        for d in (1, 2, 3):
            landed("my", 0, d - 1, my.at[(y + 4 - d) % 4])
        ml[zl] = my[0] + my[1] + my[2] + my[3]
        push("ml", 0, 0, ml.at[zl], ml.at[zl], zl_dev)
        yield
        landed("ml", 0, 0, ml.at[zlp])
        mc[co] = ml[0] + ml[1]
        push("mc", 0, 0, mc.at[co], mc.at[co], co_dev)
        yield
        landed("mc", 0, 0, mc.at[cop])
        mz[zh] = mc[0] + mc[1]
        for d in (1, 3, 2):
            push("mz", 0, d - 1, mz.at[zh], mz.at[zh], zh_dev(d))
        yield
        for d in (1, 2, 3):
            landed("mz", 0, d - 1, mz.at[(zh + 4 - d) % 4])
        mx[x] = mz[0] + mz[1] + mz[2] + mz[3]
        for d in (1, 2, 3):
            push("mx", 0, d - 1, mx.at[x], mx.at[x], x_dev(d))
        yield
        for d in (1, 2, 3):
            landed("mx", 0, d - 1, mx.at[(x + 4 - d) % 4])
        mse_ref[0, 0] = jnp.sum(mx[0] + mx[1] + mx[2] + mx[3]) / (TOKENS * DS)
        yield

    first_grad = [True]
    seen = [0] * NC
    for c in ORDER:
        if seen[c] == GAP_STAGE:
            final = c
        seen[c] += 1
    chunks = [chunk(c) for c in range(NC)]
    done = [0] * NC
    gather = student_gather()
    mse_steps = squared_total()
    for c in ORDER:
        next(chunks[c])
        if c == 0 and done[0] in GATHER_AT:
            next(gather, None)
        done[c] += 1
    for _ in mse_steps:
        pass
    for copy in started:
        copy.wait_send()


def body(teacher_attn, teacher_out_w, teacher_resid, teacher_gain, projector, student_attn, student_out_w, student_resid):
    any_spec = pl.BlockSpec(memory_space=pl.ANY)
    vmem = pltpu.VMEM
    mse, student_grad, projector_grad = pl.pallas_call(
        kernel,
        name="distill",
        out_shape=(
            jax.ShapeDtypeStruct((1, 1), F32),
            jax.ShapeDtypeStruct((KS, KS), F32),
            jax.ShapeDtypeStruct((KT, KS), F32),
        ),
        in_specs=[any_spec] * 8,
        out_specs=(
            pl.BlockSpec(memory_space=pltpu.SMEM),
            pl.BlockSpec(memory_space=vmem),
            pl.BlockSpec(memory_space=vmem),
        ),
        scratch_shapes=[
            vmem((KT, KT), BF),
            vmem((KT, KS), BF),
            vmem((KS, KS), BF),
            vmem((1, KT), F32),
            vmem((2, ROWS, KT), BF),
            vmem((ROWS, KS), BF),
            vmem((4, 2, 2, ROWS, KT), BF),
            vmem((8, ROWS, KT), BF),
            vmem((8, ROWS, KT), BF),
            vmem((8, ROWS, KT), F32),
            vmem((2, 4, ROWS, KT), BF),
            vmem((3, 2, ROWS, KT), BF),
            vmem((2, ROWS, KT), BF),
            vmem((2, ROWS, KT), BF),
            vmem((NC, 4, 8, 128), F32),
            vmem((NC, 4, 8, 128), F32),
            vmem((NC, 4, 2, 8, 128), F32),
            vmem((2, 4, 2, ROWS, KT), BF),
            vmem((2, 4, 2, ROWS, KT), BF),
            vmem((2, 4, 2, ROWS, KS), BF),
            vmem((4, 4, ROWS, KS), BF),
            vmem((3, 4, ROWS, KS), BF),
            vmem((4, ROWS, KS), F32),
            vmem((4, ROWS, KS), BF),
            vmem((3, ROWS, KS), BF),
            vmem((4, 4, ROWS, KS), BF),
            vmem((NC, 8, 128), F32),
            vmem((4, 8, 128), F32),
            vmem((4, 8, 128), F32),
            vmem((4, 8, 128), F32),
            vmem((2, 8, 128), F32),
            vmem((2, 8, 128), F32),
            pltpu.SemaphoreType.DMA((TOTAL,)),
            pltpu.SemaphoreType.DMA((TOTAL,)),
            pltpu.SemaphoreType.DMA((LOADS,)),
        ],
        compiler_params=pltpu.CompilerParams(
            collective_id=1, has_side_effects=True, vmem_limit_bytes=60 * 1024 * 1024
        ),
    )(
        teacher_attn,
        teacher_out_w,
        teacher_resid.reshape(2, 8, ROWS, KT),
        teacher_gain.reshape(1, KT),
        projector,
        student_attn,
        student_out_w,
        student_resid,
    )
    return (mse.reshape(()), student_grad, projector_grad)


def solution(mesh):
    in_specs = (
        P("seq", "tp"),
        P("tp", "seq"),
        P(None, "seq"),
        P("seq"),
        P("seq", "tp"),
        P("tp", "seq"),
        P("seq", "tp"),
        P("seq", "tp"),
    )
    out_specs = (P(), P("seq", "tp"), P("seq", "tp"))
    return jax.shard_map(body, mesh=mesh, in_specs=in_specs, out_specs=out_specs, check_vma=False)
```

profile of v0, /device:TPU:1, one launch (start us, length us, event | category | flops | bytes accessed | tf_op | source)
XLA Modules:
  0.0 137.7 jit_solution(4472717600109295427)
XLA Ops:
  0.6 131.5 %distill.1 = (f32[1,1]{1,0:T(1,128)}, f32[512,512]{1,0:T(8,128)}, f32[1024,512]{1,0:T(8,128)}) custom-call(bf16[128,1024]{1,0:T(8,128)(2,1)} %ta.1, bf16[1024,1024]{1,0:T(8,128)(2,1)} %w1_hbm.1, bf16[2,8,128,1024]{3,2,1,0:T(8,128)(2,1)} %bitcast.3, f32[1,1024]{1,0:T(1,128)} %bitcast.4, bf16[1024,512]{1,0:T(8,128)(2,1)} %pj_hbm.1, bf16[128,512]{1,0:T(8,128)(2,1)} %sa_hbm.1, ...), custom_call_target="tpu_custom_call" | custom-call | tf_op jit(solution)/shard_map/distill/pallas_call | solution.py:426
  132.1 0.0 copy-start
  133.0 2.3 %copy.15 = f32[512,512]{1,0:T(8,128)} copy(f32[512,512]{1,0:T(8,128)} %get-tuple-element.13) | data formatting | bytes 2097152
  135.2 0.0 copy-done
  135.2 1.3 copy.16
Async XLA Ops:
  132.1 3.1 %copy-start = (f32[1024,512]{1,0:T(8,128)S(1)}, f32[1024,512]{1,0:T(8,128)}, u32[]{:S(2)}) copy-start(f32[1024,512]{1,0:T(8,128)} %get-tuple-element.14) | copy-start | bytes 6291460
where the time goes:
time: 138 us
  Pallas kernels  131 us (95%)
  local copies, waits for them, and re-layouts  3.59 us (3%)
  between operations  2.62 us (2%)
    pallas_call x1, Pallas kernels, body(): pl.pallas_call(kernel, name='distill', out_shape=(jax.ShapeDtypeStruct((1...  131 us
    unnamed x4, local copies, waits for them, and re-layouts  3.59 us

commit v1 on v0

--- a/solution.py
+++ b/solution.py
@@ -341,13 +341,13 @@
         yield
         if c == final:
             next(mse_steps)
-            next(mse_steps)
         for d in (1, 3, 2):
             landed("ez", c, d - 1, e_all.at[(zh + 4 - d) % 4, x, at_c])
         block = e_all.at[:, x, at_c]
         for d in (1, 3, 2):
             push("ex", c, d - 1, block, block, x_dev(d))
         if c == final:
+            next(mse_steps)
             next(mse_steps)
         yield
         for d in (1, 3, 2):

time: 138 us -> 138 us (level)
  no operation moved by 1% of the time
where the time goes in v1:
time: 138 us
  Pallas kernels  131 us (95%)
  local copies, waits for them, and re-layouts  3.59 us (3%)
  between operations  2.62 us (2%)
    pallas_call x1, Pallas kernels, body(): pl.pallas_call(kernel, name='distill', out_shape=(jax.ShapeDtypeStruct((1...  131 us
    unnamed x4, local copies, waits for them, and re-layouts  3.59 us

profile of v1, /device:TPU:1, one launch (start us, length us, event | category | flops | bytes accessed | tf_op | source)
XLA Modules:
  0.0 137.7 jit_solution(8838736678787765656)
XLA Ops:
  0.6 131.5 %distill.1 = (f32[1,1]{1,0:T(1,128)}, f32[512,512]{1,0:T(8,128)}, f32[1024,512]{1,0:T(8,128)}) custom-call(bf16[128,1024]{1,0:T(8,128)(2,1)} %ta.1, bf16[1024,1024]{1,0:T(8,128)(2,1)} %w1_hbm.1, bf16[2,8,128,1024]{3,2,1,0:T(8,128)(2,1)} %bitcast.3, f32[1,1024]{1,0:T(1,128)} %bitcast.4, bf16[1024,512]{1,0:T(8,128)(2,1)} %pj_hbm.1, bf16[128,512]{1,0:T(8,128)(2,1)} %sa_hbm.1, ...), custom_call_target="tpu_custom_call" | custom-call | tf_op jit(solution)/shard_map/distill/pallas_call | solution.py:426
  132.1 0.0 copy-start
  133.0 2.3 %copy.15 = f32[512,512]{1,0:T(8,128)} copy(f32[512,512]{1,0:T(8,128)} %get-tuple-element.13) | data formatting | bytes 2097152
  135.2 0.0 copy-done
  135.2 1.3 copy.16
Async XLA Ops:
  132.1 3.1 %copy-start = (f32[1024,512]{1,0:T(8,128)S(1)}, f32[1024,512]{1,0:T(8,128)}, u32[]{:S(2)}) copy-start(f32[1024,512]{1,0:T(8,128)} %get-tuple-element.14) | copy-start | bytes 6291460
